TPU v7x, 32 devices: a whole 2x2x4 slice. The times are simulated.
32 devices in a mesh: rows: 4 (over y, x), batch: 8 (over z, core).
Axes of the slice: x: 2, y: 2, z: 4, core: 2. Of those that a mesh axis runs over, the one named last changes fastest.
Arguments:
- pixels: float32 [64, 32, 32, 3], P('batch', 'rows'), may hold values from 0 to 256
- valid: int32 [64, 32, 32], P('batch', 'rows'), may hold values from 0 to 1, as said below
- entry_conv: float32 [2, 3, 3, 6, 64], replicated, may hold values from -0.875 to 0.875
- entry_first: float32 [2, 3, 3, 6, 64], replicated, may hold values from -0.0068359375 to 0.0068359375
- entry_second: float32 [2, 3, 3, 6, 64], replicated, may hold values from 1.525879e-08 to 6.103516e-08
- block_conv: float32 [2, 2, 2, 3, 3, 64, 64], replicated, may hold values from -0.25 to 0.25
- block_first: float32 [2, 2, 2, 3, 3, 64, 64], replicated, may hold values from -0.0068359375 to 0.0068359375
- block_second: float32 [2, 2, 2, 3, 3, 64, 64], replicated, may hold values from 1.525879e-08 to 6.103516e-08
- exit_one: float32 [3, 3, 64, 6], replicated, may hold values from -0.25 to 0.25
- exit_one_first: float32 [3, 3, 64, 6], replicated, may hold values from -0.0068359375 to 0.0068359375
- exit_one_second: float32 [3, 3, 64, 6], replicated, may hold values from 1.525879e-08 to 6.103516e-08
- exit_two: float32 [3, 3, 64, 12], replicated, may hold values from -0.25 to 0.25
- exit_two_first: float32 [3, 3, 64, 12], replicated, may hold values from -0.0068359375 to 0.0068359375
- exit_two_second: float32 [3, 3, 64, 12], replicated, may hold values from 1.525879e-08 to 6.103516e-08
- norm_params: float32 [2, 5, 2, 64], replicated, may hold values from 0.5 to 1.5
- norm_first: float32 [2, 5, 2, 64], replicated, may hold values from -0.015625 to 0.015625
- norm_second: float32 [2, 5, 2, 64], replicated, may hold values from 1.2207032e-07 to 4.882813e-07
- head_params: float32 [27], replicated, may hold values from -1.5 to 1.5
- head_first: float32 [27], replicated, may hold values from -0.4375 to 0.4375
- head_second: float32 [27], replicated, may hold values from 0.0001 to 0.0004
Outputs:
- loss_sum: float32 [], replicated
- valid_count: float32 [], replicated
- entry_new: float32 [2, 3, 3, 6, 64], replicated
- entry_first_new: float32 [2, 3, 3, 6, 64], replicated
- entry_second_new: float32 [2, 3, 3, 6, 64], replicated
- entry_copy: bfloat16 [2, 3, 3, 6, 64], replicated
- block_new: float32 [2, 2, 2, 3, 3, 64, 64], replicated
- block_first_new: float32 [2, 2, 2, 3, 3, 64, 64], replicated
- block_second_new: float32 [2, 2, 2, 3, 3, 64, 64], replicated
- block_copy: bfloat16 [2, 2, 2, 3, 3, 64, 64], replicated
- exit_one_new: float32 [3, 3, 64, 6], replicated
- exit_one_first_new: float32 [3, 3, 64, 6], replicated
- exit_one_second_new: float32 [3, 3, 64, 6], replicated
- exit_one_copy: bfloat16 [3, 3, 64, 6], replicated
- exit_two_new: float32 [3, 3, 64, 12], replicated
- exit_two_first_new: float32 [3, 3, 64, 12], replicated
- exit_two_second_new: float32 [3, 3, 64, 12], replicated
- exit_two_copy: bfloat16 [3, 3, 64, 12], replicated
- norm_new: float32 [2, 5, 2, 64], replicated
- norm_first_new: float32 [2, 5, 2, 64], replicated
- norm_second_new: float32 [2, 5, 2, 64], replicated
- norm_copy: bfloat16 [2, 5, 2, 64], replicated
- head_new: float32 [27], replicated
- head_first_new: float32 [27], replicated
- head_second_new: float32 [27], replicated
- head_copy: bfloat16 [27], replicated
Inputs may be any that keep to these rules, and one draw needn't show every extreme that they name: `valid`: each image's ones form one rectangle of at least 4 rows and 16 columns.
All inputs are finite; a program needn't handle non-finite values.
Results may differ from a plain program's by a relative error of at most 0.012.
The roundings to bfloat16 on the way count: a program that leaves them out, or rounds other values in their place, can miss the bound.
Values may be sent and summed in bfloat16 or wider, within the bound.
No kernel may reach another device: no remote copies, remote signals or barrier semaphores. Data moves between devices by JAX's collectives and lax.ppermute only.
A program may use at most 192 MiB of HBM per device.

v0:
```python
import math

import jax
import jax.numpy as jnp
from jax import lax
from jax.sharding import PartitionSpec as P

STEP = 10


ALPHA = 0.05
NORM_EPS = 1e-05
BETA_ONE = 0.9
BETA_TWO = 0.999
ADAM_EPS = 1e-08
DECAY = 0.01
RATE_CONV = 1.0
RATE_SMALL = 10.0
LOG_TWO = math.log(2.0)
HALF_LOG_TAU = 0.5 * math.log(2.0 * math.pi)
LOG_LEVELS = math.log(256.0)


def extended(cells, sides, width):
    for axis, dim in sides:
        count = lax.axis_size(axis)
        ends = count - 1
        head = lax.slice_in_dim(cells, 0, width, axis=dim)
        tail = lax.slice_in_dim(cells, cells.shape[dim] - width, cells.shape[dim], axis=dim)
        cells = jnp.concatenate(
            [
                lax.ppermute(tail, axis, [(i, (i + 1) % count) for i in range(ends)]),
                cells,
                lax.ppermute(head, axis, [((i + 1) % count, i) for i in range(ends)]),
            ],
            axis=dim,
        )
    return cells


def squeeze(array):
    batch_n, height, columns, channels = array.shape
    grouped = array.reshape(batch_n, height // 2, 2, columns // 2, 2, channels).transpose(
        0, 1, 3, 2, 4, 5
    )
    return grouped.reshape(batch_n, height // 2, columns // 2, 4 * channels)


def unsqueeze(array):
    batch_n, height, columns, channels = array.shape
    grouped = array.reshape(batch_n, height, columns, 2, 2, channels // 4).transpose(
        0, 1, 3, 2, 4, 5
    )
    return grouped.reshape(batch_n, 2 * height, 2 * columns, channels // 4)


def widen(padded):
    return jnp.pad(padded, ((0, 0), (0, 0), (1, 1), (0, 0)))


def local_conv(padded, kernel):
    return lax.conv_general_dilated(
        widen(padded),
        kernel,
        (1, 1),
        "VALID",
        dimension_numbers=("NHWC", "HWIO", "NHWC"),
        preferred_element_type=jnp.float32,
    )


def conv_forward(inputs, kernel):
    padded = extended(inputs, (("rows", 1),), 1)
    return (local_conv(padded, kernel), padded)


def conv_backward(padded, kernel, grad_out, need_input, extra):
    grad_low = grad_out.astype(jnp.bfloat16)
    wide = widen(padded)
    height = grad_low.shape[1]
    columns = grad_low.shape[2]
    kernel_grad = jnp.stack(
        [
            jnp.stack(
                [
                    jnp.einsum(
                        "nhwi,nhwo->io",
                        wide[:, row_shift : row_shift + height, col_shift : col_shift + columns],
                        grad_low,
                        preferred_element_type=jnp.float32,
                    )
                    for col_shift in range(3)
                ]
            )
            for row_shift in range(3)
        ]
    )
    grad_in = None
    if need_input:
        grad_pad = extended(grad_low, (("rows", 1),), 1)
        grad_in = local_conv(grad_pad, jnp.flip(kernel, (0, 1)).transpose(0, 1, 3, 2))
    return (kernel_grad, grad_in, extra)


def cell_total(value):
    return (
        value.shape[0]
        * value.shape[1]
        * value.shape[2]
        * lax.axis_size("rows")
        * lax.axis_size("batch")
    )


def norm_forward(value, params):
    cells = cell_total(value)
    average = lax.psum(jnp.sum(value, axis=(0, 1, 2)), ("rows", "batch")) / cells
    centered = value - average
    variance = lax.psum(jnp.sum(centered * centered, axis=(0, 1, 2)), ("rows", "batch")) / cells
    inv_std = lax.rsqrt(variance + NORM_EPS)
    normed = centered * inv_std
    return (jax.nn.silu(normed * params[0] + params[1]).astype(jnp.bfloat16), (normed, inv_std))


def norm_backward(grad_act, stored, params):
    normed, inv_std = stored
    affine = normed * params[0] + params[1]
    sigmoid_val = jax.nn.sigmoid(affine)
    grad_affine = grad_act * sigmoid_val * (1.0 + affine * (1.0 - sigmoid_val))
    shift_grad, gain_grad = lax.psum(
        (jnp.sum(grad_affine, axis=(0, 1, 2)), jnp.sum(grad_affine * normed, axis=(0, 1, 2))),
        ("rows", "batch"),
    )
    cells = cell_total(grad_act)
    grad_in = params[0] * inv_std * (grad_affine - shift_grad / cells - normed * gain_grad / cells)
    return (grad_in, jnp.stack([gain_grad, shift_grad]))


def net_forward(inputs, entry, blocks, exit_kernel, norms, bias):
    hidden, entry_pad = conv_forward(inputs.astype(jnp.bfloat16), entry.astype(jnp.bfloat16))
    stored_blocks = []
    for block_index in range(blocks.shape[0]):
        act_one, norm_one = norm_forward(hidden, norms[2 * block_index])
        middle, pad_one = conv_forward(act_one, blocks[block_index, 0].astype(jnp.bfloat16))
        act_two, norm_two = norm_forward(middle, norms[2 * block_index + 1])
        branch, pad_two = conv_forward(act_two, blocks[block_index, 1].astype(jnp.bfloat16))
        hidden = hidden + branch
        stored_blocks.append((norm_one, pad_one, norm_two, pad_two))
    act_last, norm_last = norm_forward(hidden, norms[-1])
    result, last_pad = conv_forward(act_last, exit_kernel.astype(jnp.bfloat16))
    return (result + bias, (entry_pad, stored_blocks, norm_last, last_pad))


def net_backward(grad_out, stored, entry, blocks, exit_kernel, norms, need_input, head_extra):
    entry_pad, stored_blocks, norm_last, last_pad = stored
    exit_grad, grad_act, head_extra = conv_backward(
        last_pad, exit_kernel.astype(jnp.bfloat16), grad_out, True, head_extra
    )
    grad_hidden, last_norm_grad = norm_backward(grad_act, norm_last, norms[-1])
    block_grads = [None] * blocks.shape[0]
    norm_grads = [None] * norms.shape[0]
    norm_grads[-1] = last_norm_grad
    for block_index in reversed(range(blocks.shape[0])):
        norm_one, pad_one, norm_two, pad_two = stored_blocks[block_index]
        second_grad, grad_two, unused_two = conv_backward(
            pad_two, blocks[block_index, 1].astype(jnp.bfloat16), grad_hidden, True, None
        )
        grad_middle, norm_grads[2 * block_index + 1] = norm_backward(
            grad_two, norm_two, norms[2 * block_index + 1]
        )
        first_grad, grad_one, unused_one = conv_backward(
            pad_one, blocks[block_index, 0].astype(jnp.bfloat16), grad_middle, True, None
        )
        grad_part, norm_grads[2 * block_index] = norm_backward(
            grad_one, norm_one, norms[2 * block_index]
        )
        grad_hidden = grad_hidden + grad_part
        block_grads[block_index] = jnp.stack([first_grad, second_grad])
    entry_grad, input_grad, unused_entry = conv_backward(
        entry_pad, entry.astype(jnp.bfloat16), grad_hidden, need_input, None
    )
    return (
        entry_grad,
        jnp.stack(block_grads),
        exit_grad,
        jnp.stack(norm_grads),
        head_extra,
        input_grad,
    )


def adamw(master, first, second, grad, rate):
    first_new = BETA_ONE * first + (1.0 - BETA_ONE) * grad
    second_new = BETA_TWO * second + (1.0 - BETA_TWO) * grad * grad
    direction = (
        first_new
        / (1.0 - BETA_ONE**STEP)
        / (jnp.sqrt(second_new / (1.0 - BETA_TWO**STEP)) + ADAM_EPS)
    )
    master_new = master - rate * (direction + DECAY * master)
    return (master_new, first_new, second_new, master_new.astype(jnp.bfloat16))


def body(
    pixels,
    valid,
    entry_conv,
    entry_first,
    entry_second,
    block_conv,
    block_first,
    block_second,
    exit_one,
    exit_one_first,
    exit_one_second,
    exit_two,
    exit_two_first,
    exit_two_second,
    norm_params,
    norm_first,
    norm_second,
    head_params,
    head_first,
    head_second,
):
    chans = pixels.shape[3]
    valid_float = valid.astype(jnp.float32)
    offset = lax.axis_index("rows") * pixels.shape[1]
    band = pixels.shape[1]
    rowpos = offset + jnp.arange(band, dtype=jnp.int32)[:, None]
    colpos = jnp.arange(pixels.shape[2], dtype=jnp.int32)[None, :]
    parity = ((rowpos + colpos) % 2 == 0).astype(jnp.float32)[None, :, :, None]
    scaled = pixels / 256.0
    prob = ALPHA + (1.0 - 2.0 * ALPHA) * scaled
    logits = jnp.log(prob) - jnp.log(1.0 - prob)
    jacobian = squeeze(math.log(1.0 - 2.0 * ALPHA) - jnp.log(prob) - jnp.log(1.0 - prob))
    dim_mask = squeeze(jnp.broadcast_to(valid_float[..., None], logits.shape))
    first_in = jnp.concatenate([logits * parity, jnp.broadcast_to(parity, logits.shape)], axis=3)
    out_one, stored_one = net_forward(
        first_in,
        entry_conv[0],
        block_conv[0],
        exit_one,
        norm_params[0],
        head_params[3 * chans : 5 * chans],
    )
    tanh_one = jnp.tanh(out_one[..., :chans])
    scale_one = head_params[0:chans] * tanh_one
    exp_one = jnp.exp(scale_one)
    coupled = logits * parity + (1.0 - parity) * (logits * exp_one + out_one[..., chans:])
    squeezed = squeeze(coupled)
    logdet = squeeze((1.0 - parity) * scale_one)
    first_half = squeezed[..., : 2 * chans]
    second_half = squeezed[..., 2 * chans :]
    out_two, stored_two = net_forward(
        first_half,
        entry_conv[1],
        block_conv[1],
        exit_two,
        norm_params[1],
        head_params[5 * chans : 9 * chans],
    )
    tanh_two = jnp.tanh(out_two[..., : 2 * chans])
    scale_two = head_params[chans : 3 * chans] * tanh_two
    exp_two = jnp.exp(scale_two)
    latent = jnp.concatenate(
        [first_half, second_half * exp_two + out_two[..., 2 * chans :]], axis=3
    )
    logdet = logdet + jnp.concatenate([jnp.zeros_like(scale_two), scale_two], axis=3)
    neg_loglik = 0.5 * latent * latent + HALF_LOG_TAU - logdet - jacobian + LOG_LEVELS
    loss_total, total_valid = lax.psum(
        (jnp.sum(dim_mask * neg_loglik) / LOG_TWO, jnp.sum(dim_mask)), ("rows", "batch")
    )
    grad_nll = dim_mask / (LOG_TWO * total_valid)
    grad_latent = grad_nll * latent
    grad_moved = grad_latent[..., 2 * chans :]
    grad_scale_two = grad_moved * second_half * exp_two - grad_nll[..., 2 * chans :]
    grad_raw_two = grad_scale_two * head_params[chans : 3 * chans] * (1.0 - tanh_two * tanh_two)
    grad_out_two = jnp.concatenate([grad_raw_two, grad_moved], axis=3)
    extra_two = jnp.concatenate(
        [jnp.sum(grad_scale_two * tanh_two, axis=(0, 1, 2)), jnp.sum(grad_out_two, axis=(0, 1, 2))]
    )
    entry_two, blocks_two, exit_two_grad, norms_two, extra_two, grad_first_net = net_backward(
        grad_out_two,
        stored_two,
        entry_conv[1],
        block_conv[1],
        exit_two,
        norm_params[1],
        True,
        extra_two,
    )
    grad_squeezed = jnp.concatenate(
        [grad_latent[..., : 2 * chans] + grad_first_net, grad_moved * exp_two], axis=3
    )
    grad_coupled = unsqueeze(grad_squeezed)
    grad_logdet = unsqueeze(-grad_nll)
    grad_scale_one = (1.0 - parity) * (grad_coupled * logits * exp_one + grad_logdet)
    grad_shift_one = (1.0 - parity) * grad_coupled
    grad_raw_one = grad_scale_one * head_params[0:chans] * (1.0 - tanh_one * tanh_one)
    grad_out_one = jnp.concatenate([grad_raw_one, grad_shift_one], axis=3)
    extra_one = jnp.concatenate(
        [jnp.sum(grad_scale_one * tanh_one, axis=(0, 1, 2)), jnp.sum(grad_out_one, axis=(0, 1, 2))]
    )
    entry_one, blocks_one, exit_one_grad, norms_one, extra_one, unused_input = net_backward(
        grad_out_one,
        stored_one,
        entry_conv[0],
        block_conv[0],
        exit_one,
        norm_params[0],
        False,
        extra_one,
    )
    entry_grad = jnp.stack([entry_one, entry_two])
    block_grad = jnp.stack([blocks_one, blocks_two])
    norm_grad = jnp.stack([norms_one, norms_two])
    head_grad = jnp.concatenate(
        [extra_one[:chans], extra_two[: 2 * chans], extra_one[chans:], extra_two[2 * chans :]]
    )
    entry_grad, block_grad, exit_one_grad, exit_two_grad, head_grad = lax.psum(
        (entry_grad, block_grad, exit_one_grad, exit_two_grad, head_grad), ("rows", "batch")
    )
    entry_out = adamw(entry_conv, entry_first, entry_second, entry_grad, RATE_CONV)
    block_out = adamw(block_conv, block_first, block_second, block_grad, RATE_CONV)
    exit_a_out = adamw(exit_one, exit_one_first, exit_one_second, exit_one_grad, RATE_CONV)
    exit_b_out = adamw(exit_two, exit_two_first, exit_two_second, exit_two_grad, RATE_CONV)
    norm_out = adamw(norm_params, norm_first, norm_second, norm_grad, RATE_SMALL)
    head_out = adamw(head_params, head_first, head_second, head_grad, RATE_SMALL)
    return (
        loss_total,
        total_valid,
        entry_out[0],
        entry_out[1],
        entry_out[2],
        entry_out[3],
        block_out[0],
        block_out[1],
        block_out[2],
        block_out[3],
        exit_a_out[0],
        exit_a_out[1],
        exit_a_out[2],
        exit_a_out[3],
        exit_b_out[0],
        exit_b_out[1],
        exit_b_out[2],
        exit_b_out[3],
        norm_out[0],
        norm_out[1],
        norm_out[2],
        norm_out[3],
        head_out[0],
        head_out[1],
        head_out[2],
        head_out[3],
    )


def solution(mesh):
    placed = (
        P("batch", "rows", None, None),
        P("batch", "rows", None),
        P(),
        P(),
        P(),
        P(),
        P(),
        P(),
        P(),
        P(),
        P(),
        P(),
        P(),
        P(),
        P(),
        P(),
        P(),
        P(),
        P(),
        P(),
    )
    return jax.shard_map(
        body,
        mesh=mesh,
        in_specs=placed,
        out_specs=(
            P(),
            P(),
            P(),
            P(),
            P(),
            P(),
            P(),
            P(),
            P(),
            P(),
            P(),
            P(),
            P(),
            P(),
            P(),
            P(),
            P(),
            P(),
            P(),
            P(),
            P(),
            P(),
            P(),
            P(),
            P(),
            P(),
        ),
        check_vma=False,
    )
```

profile of v0, /device:TPU:0, one launch (start us, length us, event | category | flops | bytes accessed | tf_op | source)
XLA Modules:
  0.0 1783.7 jit_solution(3748044508605241179)
XLA Ops:
  9.7 5.5 collective-permute-start
  27.5 40.5 %psum.329 = f32[64]{0:T(128)S(1)} all-reduce(f32[64]{0:T(128)S(1)} %get-tuple-element.413), channel_id=1, replica_groups=mesh['rows'=4,'batch'=8] {'rows','batch'}, use_global_device_ids=true, to_apply=%region_1.2 | all-reduce | flops 64 | bytes 512 | tf_op jit(solution)/shard_map/psum | solution.py:117
  68.3 41.5 %psum.330 = f32[64]{0:T(128)S(1)} all-reduce(f32[64]{0:T(128)S(1)} %multiply_reduce_fusion.9), channel_id=1, replica_groups=mesh['rows'=4,'batch'=8] {'rows','batch'}, use_global_device_ids=true, to_apply=%region_3.4 | all-reduce | flops 64 | bytes 512 | tf_op jit(solution)/shard_map/psum | solution.py:119
  111.5 4.8 collective-permute-start.2
  120.0 41.0 %psum.331 = f32[64]{0:T(128)S(1)} all-reduce(f32[64]{0:T(128)S(1)} %get-tuple-element.415), channel_id=1, replica_groups=mesh['rows'=4,'batch'=8] {'rows','batch'}, use_global_device_ids=true, to_apply=%region_5.6 | all-reduce | flops 64 | bytes 512 | tf_op jit(solution)/shard_map/psum | solution.py:117
  161.4 41.4 %psum.332 = f32[64]{0:T(128)S(1)} all-reduce(f32[64]{0:T(128)S(1)} %multiply_reduce_fusion.8), channel_id=1, replica_groups=mesh['rows'=4,'batch'=8] {'rows','batch'}, use_global_device_ids=true, to_apply=%region_7.8 | all-reduce | flops 64 | bytes 512 | tf_op jit(solution)/shard_map/psum | solution.py:119
  205.0 4.8 collective-permute-start.4
  215.0 39.6 %psum.333 = f32[64]{0:T(128)S(1)} all-reduce(f32[64]{0:T(128)S(1)} %get-tuple-element.417), channel_id=1, replica_groups=mesh['rows'=4,'batch'=8] {'rows','batch'}, use_global_device_ids=true, to_apply=%region_9.10 | all-reduce | flops 64 | bytes 512 | tf_op jit(solution)/shard_map/psum | solution.py:117
  255.0 41.8 %psum.334 = f32[64]{0:T(128)S(1)} all-reduce(f32[64]{0:T(128)S(1)} %multiply_reduce_fusion.7), channel_id=1, replica_groups=mesh['rows'=4,'batch'=8] {'rows','batch'}, use_global_device_ids=true, to_apply=%region_11.12 | all-reduce | flops 64 | bytes 512 | tf_op jit(solution)/shard_map/psum | solution.py:119
  298.6 4.8 collective-permute-start.6
  308.6 39.6 %psum.335 = f32[64]{0:T(128)S(1)} all-reduce(f32[64]{0:T(128)S(1)} %get-tuple-element.419), channel_id=1, replica_groups=mesh['rows'=4,'batch'=8] {'rows','batch'}, use_global_device_ids=true, to_apply=%region_13.14 | all-reduce | flops 64 | bytes 512 | tf_op jit(solution)/shard_map/psum | solution.py:117
  348.5 41.4 %psum.336 = f32[64]{0:T(128)S(1)} all-reduce(f32[64]{0:T(128)S(1)} %multiply_reduce_fusion.6), channel_id=1, replica_groups=mesh['rows'=4,'batch'=8] {'rows','batch'}, use_global_device_ids=true, to_apply=%region_15.16 | all-reduce | flops 64 | bytes 512 | tf_op jit(solution)/shard_map/psum | solution.py:119
  391.7 4.8 collective-permute-start.8
  401.8 39.4 %psum.337 = f32[64]{0:T(128)S(1)} all-reduce(f32[64]{0:T(128)S(1)} %get-tuple-element.421), channel_id=1, replica_groups=mesh['rows'=4,'batch'=8] {'rows','batch'}, use_global_device_ids=true, to_apply=%region_17.18 | all-reduce | flops 64 | bytes 512 | tf_op jit(solution)/shard_map/psum | solution.py:117
  441.5 41.4 %psum.338 = f32[64]{0:T(128)S(1)} all-reduce(f32[64]{0:T(128)S(1)} %multiply_reduce_fusion.5), channel_id=1, replica_groups=mesh['rows'=4,'batch'=8] {'rows','batch'}, use_global_device_ids=true, to_apply=%region_19.20 | all-reduce | flops 64 | bytes 512 | tf_op jit(solution)/shard_map/psum | solution.py:119
  485.2 5.0 collective-permute-start.10
  494.8 12.4 fusion.231
  513.9 5.4 collective-permute-start.12
  526.2 39.7 %psum.339 = f32[64]{0:T(128)S(1)} all-reduce(f32[64]{0:T(128)S(1)} %get-tuple-element.423), channel_id=1, replica_groups=mesh['rows'=4,'batch'=8] {'rows','batch'}, use_global_device_ids=true, to_apply=%region_21.22 | all-reduce | flops 64 | bytes 512 | tf_op jit(solution)/shard_map/psum | solution.py:117
  566.0 41.4 %psum.340 = f32[64]{0:T(128)} all-reduce(f32[64]{0:T(128)S(1)} %multiply_reduce_fusion.19), channel_id=1, replica_groups=mesh['rows'=4,'batch'=8] {'rows','batch'}, use_global_device_ids=true, to_apply=%region_23.24 | all-reduce | flops 64 | bytes 512 | tf_op jit(solution)/shard_map/psum | solution.py:119
  610.1 4.8 collective-permute-start.14
  615.0 4.5 pad_slice_fusion.5
  621.5 39.2 %psum.341 = f32[64]{0:T(128)} all-reduce(f32[64]{0:T(128)S(1)} %get-tuple-element.425), channel_id=1, replica_groups=mesh['rows'=4,'batch'=8] {'rows','batch'}, use_global_device_ids=true, to_apply=%region_25.26 | all-reduce | flops 64 | bytes 512 | tf_op jit(solution)/shard_map/psum | solution.py:117
  662.9 41.9 %psum.342 = f32[64]{0:T(128)} all-reduce(f32[64]{0:T(128)} %multiply_reduce_fusion.18), channel_id=1, replica_groups=mesh['rows'=4,'batch'=8] {'rows','batch'}, use_global_device_ids=true, to_apply=%region_27.28 | all-reduce | flops 64 | bytes 512 | tf_op jit(solution)/shard_map/psum | solution.py:119
  709.1 5.4 collective-permute-start.16
  727.1 38.6 %psum.343 = f32[64]{0:T(128)S(1)} all-reduce(f32[64]{0:T(128)S(1)} %get-tuple-element.427), channel_id=1, replica_groups=mesh['rows'=4,'batch'=8] {'rows','batch'}, use_global_device_ids=true, to_apply=%region_29.30 | all-reduce | flops 64 | bytes 512 | tf_op jit(solution)/shard_map/psum | solution.py:117
  766.7 41.4 %psum.344 = f32[64]{0:T(128)S(1)} all-reduce(f32[64]{0:T(128)S(1)} %multiply_reduce_fusion.17), channel_id=1, replica_groups=mesh['rows'=4,'batch'=8] {'rows','batch'}, use_global_device_ids=true, to_apply=%region_31.32 | all-reduce | flops 64 | bytes 512 | tf_op jit(solution)/shard_map/psum | solution.py:119
  810.6 4.8 collective-permute-start.18
  818.3 41.0 %psum.345 = f32[64]{0:T(128)S(1)} all-reduce(f32[64]{0:T(128)S(1)} %get-tuple-element.429), channel_id=1, replica_groups=mesh['rows'=4,'batch'=8] {'rows','batch'}, use_global_device_ids=true, to_apply=%region_33.34 | all-reduce | flops 64 | bytes 512 | tf_op jit(solution)/shard_map/psum | solution.py:117
  859.4 41.4 %psum.346 = f32[64]{0:T(128)S(1)} all-reduce(f32[64]{0:T(128)S(1)} %multiply_reduce_fusion.16), channel_id=1, replica_groups=mesh['rows'=4,'batch'=8] {'rows','batch'}, use_global_device_ids=true, to_apply=%region_35.36 | all-reduce | flops 64 | bytes 512 | tf_op jit(solution)/shard_map/psum | solution.py:119
  903.6 5.4 collective-permute-start.20
  925.1 38.8 %psum.347 = f32[64]{0:T(128)S(1)} all-reduce(f32[64]{0:T(128)} %get-tuple-element.431), channel_id=1, replica_groups=mesh['rows'=4,'batch'=8] {'rows','batch'}, use_global_device_ids=true, to_apply=%region_37.38 | all-reduce | flops 64 | bytes 512 | tf_op jit(solution)/shard_map/psum | solution.py:117
  964.0 41.6 %all-reduce.24 = (f32[64]{0:T(128)S(1)}, f32[]{:T(128)}) all-reduce(f32[64]{0:T(128)S(1)} %multiply_reduce_fusion.15, f32[]{:T(128)} %broadcast_reduce_fusion), channel_id=1, replica_groups=mesh['rows'=4,'batch'=8] {'rows','batch'}, use_global_device_ids=true, to_apply=%region_39.40 | all-reduce | flops 65 | bytes 520 | tf_op jit(solution)/shard_map/psum | solution.py:119
  1010.1 5.4 collective-permute-start.22
  1030.1 5.4 collective-permute-start.24
  1048.2 3.2 fusion.279
  1051.4 40.0 %all-reduce.23 = (f32[64]{0:T(128)}, f32[64]{0:T(128)}) all-reduce(f32[64]{0:T(128)} %get-tuple-element.201, f32[64]{0:T(128)} %get-tuple-element.200), channel_id=1, replica_groups=mesh['rows'=4,'batch'=8] {'rows','batch'}, use_global_device_ids=true, to_apply=%region_47.48 | all-reduce | flops 128 | bytes 1024 | tf_op jit(solution)/shard_map/psum | solution.py:130
  1094.6 4.8 collective-permute-start.26
  1109.3 40.3 %all-reduce.22 = (f32[64]{0:T(128)}, f32[64]{0:T(128)}) all-reduce(f32[64]{0:T(128)} %get-tuple-element.199, f32[64]{0:T(128)} %get-tuple-element.198), channel_id=1, replica_groups=mesh['rows'=4,'batch'=8] {'rows','batch'}, use_global_device_ids=true, to_apply=%region_51.52 | all-reduce | flops 128 | bytes 1024 | tf_op jit(solution)/shard_map/psum | solution.py:130
  1153.0 4.8 collective-permute-start.28
  1163.6 39.6 %all-reduce.21 = (f32[64]{0:T(128)}, f32[64]{0:T(128)}) all-reduce(f32[64]{0:T(128)} %get-tuple-element.197, f32[64]{0:T(128)} %get-tuple-element.196), channel_id=1, replica_groups=mesh['rows'=4,'batch'=8] {'rows','batch'}, use_global_device_ids=true, to_apply=%region_55.56 | all-reduce | flops 128 | bytes 1024 | tf_op jit(solution)/shard_map/psum | solution.py:130
  1207.5 4.8 collective-permute-start.30
  1222.1 40.4 %all-reduce.20 = (f32[64]{0:T(128)}, f32[64]{0:T(128)}) all-reduce(f32[64]{0:T(128)} %get-tuple-element.195, f32[64]{0:T(128)} %get-tuple-element.194), channel_id=1, replica_groups=mesh['rows'=4,'batch'=8] {'rows','batch'}, use_global_device_ids=true, to_apply=%region_59.60 | all-reduce | flops 128 | bytes 1024 | tf_op jit(solution)/shard_map/psum | solution.py:130
  1265.7 4.8 collective-permute-start.32
  1277.3 39.5 %all-reduce.19 = (f32[64]{0:T(128)}, f32[64]{0:T(128)}) all-reduce(f32[64]{0:T(128)} %get-tuple-element.193, f32[64]{0:T(128)} %get-tuple-element.192), channel_id=1, replica_groups=mesh['rows'=4,'batch'=8] {'rows','batch'}, use_global_device_ids=true, to_apply=%region_63.64 | all-reduce | flops 128 | bytes 1024 | tf_op jit(solution)/shard_map/psum | solution.py:130
  1322.3 5.0 collective-permute-start.34
  1341.1 5.5 collective-permute-start.36
  1351.2 4.9 fusion.274
  1356.0 41.6 %all-reduce.18 = (f32[64]{0:T(128)S(1)}, f32[64]{0:T(128)S(1)}) all-reduce(f32[64]{0:T(128)S(1)} %get-tuple-element.191, f32[64]{0:T(128)S(1)} %get-tuple-element.190), channel_id=1, replica_groups=mesh['rows'=4,'batch'=8] {'rows','batch'}, use_global_device_ids=true, to_apply=%region_67.68 | all-reduce | flops 128 | bytes 1024 | tf_op jit(solution)/shard_map/psum | solution.py:130
  1400.9 4.8 collective-permute-start.38
  1410.5 3.7 fusion.273
  1414.2 39.2 %all-reduce.17 = (f32[64]{0:T(128)S(1)}, f32[64]{0:T(128)S(1)}) all-reduce(f32[64]{0:T(128)S(1)} %get-tuple-element.189, f32[64]{0:T(128)S(1)} %get-tuple-element.188), channel_id=1, replica_groups=mesh['rows'=4,'batch'=8] {'rows','batch'}, use_global_device_ids=true, to_apply=%region_71.72 | all-reduce | flops 128 | bytes 1024 | tf_op jit(solution)/shard_map/psum | solution.py:130
  1457.0 5.0 collective-permute-start.40
  1467.3 3.6 fusion.272
  1471.0 40.2 %all-reduce.16 = (f32[64]{0:T(128)S(1)}, f32[64]{0:T(128)S(1)}) all-reduce(f32[64]{0:T(128)S(1)} %get-tuple-element.187, f32[64]{0:T(128)S(1)} %get-tuple-element.186), channel_id=1, replica_groups=mesh['rows'=4,'batch'=8] {'rows','batch'}, use_global_device_ids=true, to_apply=%region_75.76 | all-reduce | flops 128 | bytes 1024 | tf_op jit(solution)/shard_map/psum | solution.py:130
  1511.2 3.5 fusion.293
  1516.3 4.8 collective-permute-start.42
  1525.3 3.6 fusion.271
  1529.0 39.1 %all-reduce.15 = (f32[64]{0:T(128)S(1)}, f32[64]{0:T(128)S(1)}) all-reduce(f32[64]{0:T(128)S(1)} %get-tuple-element.185, f32[64]{0:T(128)S(1)} %get-tuple-element.184), channel_id=1, replica_groups=mesh['rows'=4,'batch'=8] {'rows','batch'}, use_global_device_ids=true, to_apply=%region_79.80 | all-reduce | flops 128 | bytes 1024 | tf_op jit(solution)/shard_map/psum | solution.py:130
  1571.5 5.7 collective-permute-start.44
  1588.2 39.6 %all-reduce.14 = (f32[64]{0:T(128)S(1)}, f32[64]{0:T(128)S(1)}) all-reduce(f32[64]{0:T(128)S(1)} %get-tuple-element.183, f32[64]{0:T(128)S(1)} %get-tuple-element.182), channel_id=1, replica_groups=mesh['rows'=4,'batch'=8] {'rows','batch'}, use_global_device_ids=true, to_apply=%region_83.84 | all-reduce | flops 128 | bytes 1024 | tf_op jit(solution)/shard_map/psum | solution.py:130
  1631.9 43.9 %all-reduce.29 = (f32[]{:T(128)}, f32[2,3,3,6,64]{4,3,2,1,0:T(8,128)S(1)}, f32[3,3,64,6]{2,3,1,0:T(8,128)S(1)}, f32[3,3,64,12]{2,3,1,0:T(8,128)S(1)}, f32[27]{0:T(128)S(1)}) all-reduce(f32[]{:T(128)S(6)} %div.295, f32[2,3,3,6,64]{4,3,2,1,0:T(8,128)S(1)} %pad_maximum_fusion.34, ...), channel_id=1, replica_groups=mesh['rows'=4,'batch'=8] {'rows','batch'}, use_global_device_ids=true, to_apply=%region_41.42 | all-reduce | flops 17308 | bytes 138464 | tf_op jit(solution)/shard_map/psum | solution.py:271
  1681.3 87.0 %all-reduce.28.cloned.1.call-done = f32[2,2,2,3,3,64,64]{6,5,4,3,2,1,0:T(8,128)} async-done(((f32[2,2,2,3,3,64,64]{6,5,4,3,2,1,0:T(8,128)}), f32[2,2,2,3,3,64,64]{6,5,4,3,2,1,0:T(8,128)}) %all-reduce.28.cloned.1.call-update) | async-done | bytes 1179664 | tf_op jit(solution)/shard_map/psum | solution.py:321
  1768.3 8.1 fusion.288
  (949 shorter events, 257.1 us)
Async XLA Ops:
  7.2 1761.1 %all-reduce.28.cloned.1.call-start = ((), (), s32[]{:S(2)}) async-start(), calls=%async_computation | async-start | bytes 4718592 | tf_op jit(solution)/shard_map/psum | solution.py:321
  8.4 14.6 collective-permute-start.1
  9.7 13.3 collective-permute-start
  16.7 93.1 %copy-start.183 = (f32[64]{0:T(128)}, f32[64]{0:T(128)S(1)}, u32[]{:S(2)}) copy-start(f32[64]{0:T(128)S(1)} %get-tuple-element.404) | copy-start | bytes 772
  16.7 93.1 %copy-start.185 = (f32[64]{0:T(128)}, f32[64]{0:T(128)S(1)}, u32[]{:S(2)}) copy-start(f32[64]{0:T(128)S(1)} %get-tuple-element.405) | copy-start | bytes 772
  16.7 186.7 %copy-start.187 = (f32[64]{0:T(128)}, f32[64]{0:T(128)S(1)}, u32[]{:S(2)}) copy-start(f32[64]{0:T(128)S(1)} %get-tuple-element.402) | copy-start | bytes 772
  16.7 186.6 %copy-start.189 = (f32[64]{0:T(128)}, f32[64]{0:T(128)S(1)}, u32[]{:S(2)}) copy-start(f32[64]{0:T(128)S(1)} %get-tuple-element.403) | copy-start | bytes 772
  16.7 280.1 %copy-start.191 = (f32[64]{0:T(128)}, f32[64]{0:T(128)S(1)}, u32[]{:S(2)}) copy-start(f32[64]{0:T(128)S(1)} %get-tuple-element.400) | copy-start | bytes 772
  16.7 280.1 %copy-start.193 = (f32[64]{0:T(128)}, f32[64]{0:T(128)S(1)}, u32[]{:S(2)}) copy-start(f32[64]{0:T(128)S(1)} %get-tuple-element.401) | copy-start | bytes 772
  16.7 373.2 %copy-start.195 = (f32[64]{0:T(128)}, f32[64]{0:T(128)S(1)}, u32[]{:S(2)}) copy-start(f32[64]{0:T(128)S(1)} %get-tuple-element.398) | copy-start | bytes 772
  16.7 373.2 %copy-start.197 = (f32[64]{0:T(128)}, f32[64]{0:T(128)S(1)}, u32[]{:S(2)}) copy-start(f32[64]{0:T(128)S(1)} %get-tuple-element.399) | copy-start | bytes 772
  16.7 466.2 %copy-start.199 = (f32[64]{0:T(128)}, f32[64]{0:T(128)S(1)}, u32[]{:S(2)}) copy-start(f32[64]{0:T(128)S(1)} %get-tuple-element.396) | copy-start | bytes 772
  16.8 466.2 %copy-start.200 = (f32[64]{0:T(128)}, f32[64]{0:T(128)S(1)}, u32[]{:S(2)}) copy-start(f32[64]{0:T(128)S(1)} %get-tuple-element.397) | copy-start | bytes 772
  110.2 101.8 %copy-start.5 = (bf16[8,8,32,64]{3,0,2,1:T(8,128)(2,1)}, bf16[8,8,32,64]{3,0,2,1:T(8,128)(2,1)S(1)}, u32[]{:S(2)}) copy-start(bf16[8,8,32,64]{3,0,2,1:T(8,128)(2,1)S(1)} %multiply_convert_fusion.6) | copy-start | bytes 786436
  110.2 6.9 collective-permute-start.3
  111.5 6.7 collective-permute-start.2
  203.7 9.4 collective-permute-start.5
  205.0 8.1 collective-permute-start.4
  297.3 9.4 collective-permute-start.7
  298.6 8.2 collective-permute-start.6
  390.4 9.4 collective-permute-start.9
  391.7 8.1 collective-permute-start.8
  483.9 9.6 collective-permute-start.11
  485.2 8.4 collective-permute-start.10
  512.6 8.8 collective-permute-start.13
  513.9 7.5 collective-permute-start.12
  526.2 198.8 %copy-start.20 = (f32[8,4,16,64]{3,0,2,1:T(8,128)}, f32[8,4,16,64]{3,0,2,1:T(8,128)S(1)}, u32[]{:S(2)}) copy-start(f32[8,4,16,64]{3,0,2,1:T(8,128)S(1)} %get-tuple-element.424) | copy-start | bytes 393220
  608.8 10.6 collective-permute-start.15
  610.1 9.3 collective-permute-start.14
  619.5 86.0 %copy-start.204 = (f32[64]{0:T(128)S(1)}, f32[64]{0:T(128)}, u32[]{:S(2)}) copy-start(f32[64]{0:T(128)} %get-tuple-element.392) | copy-start | bytes 772
  707.8 17.2 collective-permute-start.17
  709.1 15.9 collective-permute-start.16
  765.7 135.9 %copy-start.153 = (f32[64]{0:T(128)}, f32[64]{0:T(128)S(1)}, u32[]{:S(2)}) copy-start(f32[64]{0:T(128)S(1)} %broadcast_multiply_fusion.8) | copy-start | bytes 772
  809.3 7.0 collective-permute-start.19
  810.6 6.4 collective-permute-start.18
  818.3 104.8 %copy-start.24 = (f32[8,4,16,64]{3,0,2,1:T(8,128)}, f32[8,4,16,64]{3,0,2,1:T(8,128)S(1)}, u32[]{:S(2)}) copy-start(f32[8,4,16,64]{3,0,2,1:T(8,128)S(1)} %get-tuple-element.430) | copy-start | bytes 393220
  902.3 20.8 %collective-permute-start.21 = (bf16[8,1,16,64]{3,0,2,1:T(8,128)(2,1)}, bf16[8,1,16,64]{3,0,2,1:T(8,128)(2,1)}, u32[]{:S(2)}, u32[]{:S(2)}) collective-permute-start(bf16[8,1,16,64]{3,0,2,1:T(8,128)(2,1)} %get-tuple-element.350), channel_id=1, source_target_pairs={{8,0},{16,8},{24,16},{9,1},{17,9},{25,17},{10,2},{18,10},{26,18},{... | collective-permute-start | bytes 49160 | tf_op jit(solution)/shard_map/ppermute | solution.py:34
  903.6 19.5 %collective-permute-start.20 = (bf16[8,1,16,64]{3,0,2,1:T(8,128)(2,1)}, bf16[8,1,16,64]{3,0,2,1:T(8,128)(2,1)}, u32[]{:S(2)}, u32[]{:S(2)}) collective-permute-start(bf16[8,1,16,64]{3,0,2,1:T(8,128)(2,1)} %get-tuple-element.349), channel_id=1, source_target_pairs={{0,8},{8,16},{16,24},{1,9},{9,17},{17,25},{2,10},{10,18},{18,26},{... | collective-permute-start | bytes 49160 | tf_op jit(solution)/shard_map/ppermute | solution.py:32
  1008.8 8.8 collective-permute-start.23
  1010.1 7.5 collective-permute-start.22
  1028.7 16.1 collective-permute-start.25
  1030.1 14.7 collective-permute-start.24
  1093.3 13.3 collective-permute-start.27
  1094.6 12.0 collective-permute-start.26
  1151.7 9.3 collective-permute-start.29
  1153.0 8.0 collective-permute-start.28
  1206.2 13.3 collective-permute-start.31
  1207.5 12.0 collective-permute-start.30
  1264.4 10.2 collective-permute-start.33
  1265.7 8.9 collective-permute-start.32
  1321.0 7.1 collective-permute-start.35
  1322.3 6.4 collective-permute-start.34
  1339.6 10.0 collective-permute-start.37
  1341.1 8.5 collective-permute-start.36
  1397.6 113.6 %copy-start.165 = (f32[64]{0:T(128)}, f32[64]{0:T(128)S(1)}, u32[]{:S(2)}) copy-start(f32[64]{0:T(128)S(1)} %get-tuple-element.215) | copy-start | bytes 772
  1399.6 10.1 collective-permute-start.39
  1400.9 8.8 collective-permute-start.38
  1455.7 11.3 collective-permute-start.41
  1457.0 10.0 collective-permute-start.40
  1515.0 10.1 collective-permute-start.43
  1516.3 8.8 collective-permute-start.42
  1570.1 15.0 collective-permute-start.45
  1571.5 13.6 collective-permute-start.44
  1631.4 137.0 %copy-start.17 = (f32[2,2,2,3,3,64,64]{6,5,4,3,2,1,0:T(8,128)S(1)}, f32[2,2,2,3,3,64,64]{6,5,4,3,2,1,0:T(8,128)}, u32[]{:S(2)}) copy-start(f32[2,2,2,3,3,64,64]{6,5,4,3,2,1,0:T(8,128)} %param.25) | copy-start | bytes 3538948
  (245 other events, 3096.2 us)
Sparse Core Ops, SparseCore 0:
  1631.5 136.7 all-reduce.27
where the time goes:
time: 1800 us; the launch traced here: 1780 us
  blocking collectives  1260 us (70%)
  starting transfers between devices  147 us (8%)
  matrix products  111 us (6%)
  waiting for transfers between devices  89.5 us (5%)
  local copies, waits for them, and re-layouts  81.8 us (5%)
  other arithmetic  78.9 us (4%)
  between operations  19.5 us (1%)
    psum x10, blocking collectives, norm_forward(): lax.psum(jnp.sum(centered * centered, axis=(0, 1, 2)), ('rows', 'batch'))  415 us
    psum x10, blocking collectives, norm_backward(): lax.psum((jnp.sum(grad_affine, axis=(0, 1, 2)), jnp.sum(grad_affine * nor...  399 us
    psum x10, blocking collectives, norm_forward(): lax.psum(jnp.sum(value, axis=(0, 1, 2)), ('rows', 'batch')) / cells  398 us
    ppermute x23, starting transfers between devices, extended(): lax.ppermute(tail, axis, [(i, (i + 1) % count) for i in range(ends)])  116 us
    psum x1, waiting for transfers between devices, body(): lax.psum((entry_grad, block_grad, exit_one_grad, exit_two_grad, head_grad...  87 us
    conv_general_dilated x23, matrix products, local_conv(): lax.conv_general_dilated(widen(padded), kernel, (1, 1), 'VALID', dimensio...  68 us
    psum x1, blocking collectives, body(): lax.psum((jnp.sum(dim_mask * neg_loglik) / LOG_TWO, jnp.sum(dim_mask)), (...  43.9 us
    dot_general x108, matrix products, conv_backward(): jnp.einsum('nhwi,nhwo->io', wide[:, row_shift:row_shift + height, col_shi...  43.3 us
  transfers between devices with their start and end apart: 47, of which 4 were waited for; matrix products, arithmetic and copies ran while one was open for 6% of the time, Pallas kernels for 0%

commit v1 on v0

v1 whole, which is shorter than its diff:
```python
import math

import jax
import jax.numpy as jnp
from jax import lax
from jax.sharding import PartitionSpec as P

STEP = 10
ALPHA = 0.05
NORM_EPS = 1e-05
BETA_ONE = 0.9
BETA_TWO = 0.999
ADAM_EPS = 1e-08
DECAY = 0.01
RATE_CONV = 1.0
RATE_SMALL = 10.0
LOG_TWO = math.log(2.0)
HALF_LOG_TAU = 0.5 * math.log(2.0 * math.pi)
LOG_LEVELS = math.log(256.0)
IMAGES = 8
BITS = (("batch", 1), ("rows", 1), ("rows", 2), ("batch", 2), ("batch", 4), ("batch", 8), ("batch", 16), ("batch", 32))


def axis_bits():
    return [bit for bit in BITS if bit[1] < lax.axis_size(bit[0])]


def group_bits(batch):
    bits = axis_bits()
    count = max(batch // IMAGES, 1).bit_length() - 1
    return bits[: min(count, len(bits))]


def swap(value, bit):
    axis, mask = bit
    return lax.ppermute(value, axis, [(i, i ^ mask) for i in range(lax.axis_size(axis))])


def side(bit):
    return (lax.axis_index(bit[0]) // bit[1]) % 2


def group_sum(value, bits):
    for bit in bits:
        value = jax.tree.map(lambda own: own + swap(own, bit), value)
    return value


def distribute(cells, group):
    for bit in sorted(axis_bits(), key=lambda b: (b[0] != "rows", b[1])):
        mine = side(bit)
        dim = 1 if bit[0] == "rows" else 0
        if bit in group:
            if bit[0] == "batch":
                continue
            half = cells.shape[0] // 2
            away = lax.dynamic_slice_in_dim(cells, (1 - mine) * half, half, 0)
            cells = lax.dynamic_slice_in_dim(cells, mine * half, half, 0)
        else:
            away = cells
        other = swap(away, bit)
        first = jnp.where(mine == 0, cells, other)
        second = jnp.where(mine == 0, other, cells)
        cells = jnp.concatenate([first, second], axis=dim)
    return cells


def squeeze(array):
    batch_n, height, columns, channels = array.shape
    grouped = array.reshape(batch_n, height // 2, 2, columns // 2, 2, channels).transpose(
        0, 1, 3, 2, 4, 5
    )
    return grouped.reshape(batch_n, height // 2, columns // 2, 4 * channels)


def unsqueeze(array):
    batch_n, height, columns, channels = array.shape
    grouped = array.reshape(batch_n, height, columns, 2, 2, channels // 4).transpose(
        0, 1, 3, 2, 4, 5
    )
    return grouped.reshape(batch_n, 2 * height, 2 * columns, channels // 4)


def conv(inputs, kernel):
    return lax.conv_general_dilated(
        inputs,
        kernel,
        (1, 1),
        "SAME",
        dimension_numbers=("NHWC", "HWIO", "NHWC"),
        preferred_element_type=jnp.float32,
    )


def conv_backward(inputs, kernel, grad_out, need_input):
    grad_low = grad_out.astype(jnp.bfloat16)
    kernel_grad = lax.conv_general_dilated(
        inputs,
        grad_low,
        (1, 1),
        ((1, 1), (1, 1)),
        dimension_numbers=("CHWN", "IHWO", "HWNC"),
        preferred_element_type=jnp.float32,
    )
    grad_in = None
    if need_input:
        grad_in = conv(grad_low, jnp.flip(kernel, (0, 1)).transpose(0, 1, 3, 2))
    return (kernel_grad, grad_in)


def norm_forward(value, params, group):
    count = value.shape[0] * value.shape[1] * value.shape[2]
    average = jnp.mean(value, axis=(0, 1, 2))
    spread = jnp.sum(jnp.square(value - average), axis=(0, 1, 2))
    both = jnp.stack([average, spread])
    for bit in group:
        other = swap(both, bit)
        gap = both[0] - other[0]
        both = jnp.stack([0.5 * (both[0] + other[0]), both[1] + other[1] + gap * gap * (0.5 * count)])
        count = 2 * count
    inv_std = lax.rsqrt(both[1] / count + NORM_EPS)
    normed = (value - both[0]) * inv_std
    return (jax.nn.silu(normed * params[0] + params[1]).astype(jnp.bfloat16), (normed, inv_std, count))


def norm_backward(grad_act, stored, params, group):
    normed, inv_std, cells = stored
    affine = normed * params[0] + params[1]
    sigmoid_val = jax.nn.sigmoid(affine)
    grad_affine = grad_act * sigmoid_val * (1.0 + affine * (1.0 - sigmoid_val))
    both = group_sum(
        jnp.stack([jnp.sum(grad_affine * normed, axis=(0, 1, 2)), jnp.sum(grad_affine, axis=(0, 1, 2))]),
        group,
    )
    grad_in = params[0] * inv_std * (grad_affine - both[1] / cells - normed * both[0] / cells)
    return (grad_in, both)


def net_forward(inputs, entry, blocks, exit_kernel, norms, bias, group):
    entry_in = inputs.astype(jnp.bfloat16)
    hidden = conv(entry_in, entry)
    stored_blocks = []
    for block_index in range(blocks.shape[0]):
        act_one, norm_one = norm_forward(hidden, norms[2 * block_index], group)
        middle = conv(act_one, blocks[block_index, 0])
        act_two, norm_two = norm_forward(middle, norms[2 * block_index + 1], group)
        hidden = hidden + conv(act_two, blocks[block_index, 1])
        stored_blocks.append((norm_one, act_one, norm_two, act_two))
    act_last, norm_last = norm_forward(hidden, norms[-1], group)
    return (conv(act_last, exit_kernel) + bias, (entry_in, stored_blocks, norm_last, act_last))


def net_backward(grad_out, stored, entry, blocks, exit_kernel, norms, need_input, group):
    entry_in, stored_blocks, norm_last, act_last = stored
    exit_grad, grad_act = conv_backward(act_last, exit_kernel, grad_out, True)
    grad_hidden, last_norm_grad = norm_backward(grad_act, norm_last, norms[-1], group)
    block_grads = [None] * blocks.shape[0]
    norm_grads = [None] * norms.shape[0]
    norm_grads[-1] = last_norm_grad
    for block_index in reversed(range(blocks.shape[0])):
        norm_one, act_one, norm_two, act_two = stored_blocks[block_index]
        second_grad, grad_two = conv_backward(act_two, blocks[block_index, 1], grad_hidden, True)
        grad_middle, norm_grads[2 * block_index + 1] = norm_backward(
            grad_two, norm_two, norms[2 * block_index + 1], group
        )
        first_grad, grad_one = conv_backward(act_one, blocks[block_index, 0], grad_middle, True)
        grad_part, norm_grads[2 * block_index] = norm_backward(
            grad_one, norm_one, norms[2 * block_index], group
        )
        grad_hidden = grad_hidden + grad_part
        block_grads[block_index] = jnp.stack([first_grad, second_grad])
    entry_grad, input_grad = conv_backward(entry_in, entry, grad_hidden, need_input)
    return (entry_grad, jnp.stack(block_grads), exit_grad, jnp.stack(norm_grads), input_grad)


def adamw(master, first, second, grad, rate):
    first_new = BETA_ONE * first + (1.0 - BETA_ONE) * grad
    second_new = BETA_TWO * second + (1.0 - BETA_TWO) * grad * grad
    direction = (
        first_new
        / (1.0 - BETA_ONE**STEP)
        / (jnp.sqrt(second_new / (1.0 - BETA_TWO**STEP)) + ADAM_EPS)
    )
    master_new = master - rate * (direction + DECAY * master)
    return (master_new, first_new, second_new, master_new.astype(jnp.bfloat16))


def body(
    pixels,
    valid,
    entry_conv,
    entry_first,
    entry_second,
    block_conv,
    block_first,
    block_second,
    exit_one,
    exit_one_first,
    exit_one_second,
    exit_two,
    exit_two_first,
    exit_two_second,
    norm_params,
    norm_first,
    norm_second,
    head_params,
    head_first,
    head_second,
):
    chans = pixels.shape[3]
    group = group_bits(pixels.shape[0] * lax.axis_size("batch"))
    cells = distribute(jnp.concatenate([pixels, valid[..., None].astype(jnp.float32)], axis=3), group)
    pixels = cells[..., :chans]
    valid_float = cells[..., chans]
    rowpos = jnp.arange(pixels.shape[1], dtype=jnp.int32)[:, None]
    colpos = jnp.arange(pixels.shape[2], dtype=jnp.int32)[None, :]
    parity = ((rowpos + colpos) % 2 == 0).astype(jnp.float32)[None, :, :, None]
    scaled = pixels / 256.0
    prob = ALPHA + (1.0 - 2.0 * ALPHA) * scaled
    logits = jnp.log(prob) - jnp.log(1.0 - prob)
    jacobian = squeeze(math.log(1.0 - 2.0 * ALPHA) - jnp.log(prob) - jnp.log(1.0 - prob))
    dim_mask = squeeze(jnp.broadcast_to(valid_float[..., None], logits.shape))
    total_valid = group_sum(jnp.sum(dim_mask)[None], group)[0]
    first_in = jnp.concatenate([logits * parity, jnp.broadcast_to(parity, logits.shape)], axis=3)
    entry_low = entry_conv.astype(jnp.bfloat16)
    block_low = block_conv.astype(jnp.bfloat16)
    exit_one_low = exit_one.astype(jnp.bfloat16)
    exit_two_low = exit_two.astype(jnp.bfloat16)
    out_one, stored_one = net_forward(
        first_in,
        entry_low[0],
        block_low[0],
        exit_one_low,
        norm_params[0],
        head_params[3 * chans : 5 * chans],
        group,
    )
    tanh_one = jnp.tanh(out_one[..., :chans])
    scale_one = head_params[0:chans] * tanh_one
    exp_one = jnp.exp(scale_one)
    coupled = logits * parity + (1.0 - parity) * (logits * exp_one + out_one[..., chans:])
    squeezed = squeeze(coupled)
    logdet = squeeze((1.0 - parity) * scale_one)
    first_half = squeezed[..., : 2 * chans]
    second_half = squeezed[..., 2 * chans :]
    out_two, stored_two = net_forward(
        first_half,
        entry_low[1],
        block_low[1],
        exit_two_low,
        norm_params[1],
        head_params[5 * chans : 9 * chans],
        group,
    )
    tanh_two = jnp.tanh(out_two[..., : 2 * chans])
    scale_two = head_params[chans : 3 * chans] * tanh_two
    exp_two = jnp.exp(scale_two)
    latent = jnp.concatenate(
        [first_half, second_half * exp_two + out_two[..., 2 * chans :]], axis=3
    )
    logdet = logdet + jnp.concatenate([jnp.zeros_like(scale_two), scale_two], axis=3)
    neg_loglik = 0.5 * latent * latent + HALF_LOG_TAU - logdet - jacobian + LOG_LEVELS
    loss_part = jnp.sum(dim_mask * neg_loglik) / LOG_TWO
    grad_nll = dim_mask / (LOG_TWO * total_valid)
    grad_latent = grad_nll * latent
    grad_moved = grad_latent[..., 2 * chans :]
    grad_scale_two = grad_moved * second_half * exp_two - grad_nll[..., 2 * chans :]
    grad_raw_two = grad_scale_two * head_params[chans : 3 * chans] * (1.0 - tanh_two * tanh_two)
    grad_out_two = jnp.concatenate([grad_raw_two, grad_moved], axis=3)
    extra_two = jnp.concatenate(
        [jnp.sum(grad_scale_two * tanh_two, axis=(0, 1, 2)), jnp.sum(grad_out_two, axis=(0, 1, 2))]
    )
    entry_two, blocks_two, exit_two_grad, norms_two, grad_first_net = net_backward(
        grad_out_two,
        stored_two,
        entry_low[1],
        block_low[1],
        exit_two_low,
        norm_params[1],
        True,
        group,
    )
    grad_squeezed = jnp.concatenate(
        [grad_latent[..., : 2 * chans] + grad_first_net, grad_moved * exp_two], axis=3
    )
    grad_coupled = unsqueeze(grad_squeezed)
    grad_logdet = unsqueeze(-grad_nll)
    grad_scale_one = (1.0 - parity) * (grad_coupled * logits * exp_one + grad_logdet)
    grad_shift_one = (1.0 - parity) * grad_coupled
    grad_raw_one = grad_scale_one * head_params[0:chans] * (1.0 - tanh_one * tanh_one)
    grad_out_one = jnp.concatenate([grad_raw_one, grad_shift_one], axis=3)
    extra_one = jnp.concatenate(
        [jnp.sum(grad_scale_one * tanh_one, axis=(0, 1, 2)), jnp.sum(grad_out_one, axis=(0, 1, 2))]
    )
    entry_one, blocks_one, exit_one_grad, norms_one, unused_input = net_backward(
        grad_out_one,
        stored_one,
        entry_low[0],
        block_low[0],
        exit_one_low,
        norm_params[0],
        False,
        group,
    )
    norm_grad = jnp.stack([norms_one, norms_two])
    head_grad = jnp.concatenate(
        [extra_one[:chans], extra_two[: 2 * chans], extra_one[chans:], extra_two[2 * chans :]]
    )
    parts = [
        jnp.stack([entry_one, entry_two]),
        jnp.stack([blocks_one, blocks_two]),
        exit_one_grad,
        exit_two_grad,
        head_grad,
        loss_part[None],
    ]
    sizes = [part.size for part in parts]
    total = sum(sizes)
    flat = jnp.concatenate([part.reshape(-1) for part in parts] + [jnp.zeros((-total % 1024,), jnp.float32)])
    flat = group_sum(flat.reshape(-1, 128), group).reshape(-1)
    grads = []
    start = 0
    for part in parts:
        grads.append(flat[start : start + part.size].reshape(part.shape))
        start += part.size
    entry_grad, block_grad, exit_one_grad, exit_two_grad, head_grad, loss_total = grads
    entry_out = adamw(entry_conv, entry_first, entry_second, entry_grad, RATE_CONV)
    block_out = adamw(block_conv, block_first, block_second, block_grad, RATE_CONV)
    exit_a_out = adamw(exit_one, exit_one_first, exit_one_second, exit_one_grad, RATE_CONV)
    exit_b_out = adamw(exit_two, exit_two_first, exit_two_second, exit_two_grad, RATE_CONV)
    norm_out = adamw(norm_params, norm_first, norm_second, norm_grad, RATE_SMALL)
    head_out = adamw(head_params, head_first, head_second, head_grad, RATE_SMALL)
    return (
        (loss_total[0], total_valid)
        + entry_out
        + block_out
        + exit_a_out
        + exit_b_out
        + norm_out
        + head_out
    )


def solution(mesh):
    placed = (P("batch", "rows", None, None), P("batch", "rows", None)) + (P(),) * 18
    return jax.shard_map(body, mesh=mesh, in_specs=placed, out_specs=(P(),) * 26, check_vma=False)
```

time: 1800 us -> 661 us (0.37)
  blocking collectives: 1260 us -> 0 us
  matrix products: 111 us -> 267 us
  starting transfers between devices: 147 us -> 71.4 us
  waiting for transfers between devices: 89.5 us -> 154 us
    psum x31 -> x0, blocking collectives: 1260 us -> none  [the longest x10 415 us: norm_forward(): lax.psum(jnp.sum(centered * centered, axis=(0, 1, 2)), ('rows', 'batch'))]
    conv_general_dilated x23 -> x35, matrix products: 68 us -> 267 us  [the longest x23 139 us: conv(): lax.conv_general_dilated(inputs, kernel, (1, 1), 'SAME', dimension_number...]
    ppermute x46 -> x70, waiting for transfers between devices: 2.46 us -> 154 us  [swap(): lax.ppermute(value, axis, [(i, i ^ mask) for i in range(lax.axis_size(axi...]
    psum x1 -> x0, waiting for transfers between devices: 87 us -> none  [body(): lax.psum((entry_grad, block_grad, exit_one_grad, exit_two_grad, head_grad...]
    ppermute x46 -> x70, starting transfers between devices: 146 us -> 71.4 us  [swap(): lax.ppermute(value, axis, [(i, i ^ mask) for i in range(lax.axis_size(axi...]
    dot_general x108 -> x0, matrix products: 43.3 us -> none  [conv_backward(): jnp.einsum('nhwi,nhwo->io', wide[:, row_shift:row_shift + height, col_shi...]
    slice x37 -> x5, local copies, waits for them, and re-layouts: 29.5 us -> 3.28 us  [the longest x1 1.93 us: body(): valid_float = cells[..., chans]]
  transfers between devices with their start and end apart: 47 -> 70, of which waited for: 4 -> 57; matrix products, arithmetic and copies ran while one was open for 6% -> 23% of each run, Pallas kernels for 0% -> 0%
where the time goes in v1:
time: 661 us; the launch traced here: 650 us
  matrix products  267 us (40%)
  waiting for transfers between devices  154 us (23%)
  local copies, waits for them, and re-layouts  77.4 us (12%)
  starting transfers between devices  71.4 us (11%)
  other arithmetic  71.1 us (11%)
  between operations  9.16 us (1%)
    ppermute x70, waiting for transfers between devices, swap(): lax.ppermute(value, axis, [(i, i ^ mask) for i in range(lax.axis_size(axi...  154 us
    conv_general_dilated x23, matrix products, conv(): lax.conv_general_dilated(inputs, kernel, (1, 1), 'SAME', dimension_number...  139 us
    conv_general_dilated x12, matrix products, conv_backward(): lax.conv_general_dilated(inputs, grad_low, (1, 1), ((1, 1), (1, 1)), dime...  128 us
    ppermute x70, starting transfers between devices, swap(): lax.ppermute(value, axis, [(i, i ^ mask) for i in range(lax.axis_size(axi...  71.4 us
    unnamed x497, local copies, waits for them, and re-layouts  20.6 us
    convert_element_type x6, other arithmetic, adamw(): return (master_new, first_new, second_new, master_new.astype(jnp.bfloat16))  14.1 us
  transfers between devices with their start and end apart: 70, of which 57 were waited for; matrix products, arithmetic and copies ran while one was open for 23% of the time, Pallas kernels for 0%

profile of v1, /device:TPU:0, one launch (start us, length us, event | category | flops | bytes accessed | tf_op | source)
XLA Modules:
  0.0 649.7 jit_solution(8759451240941963423)
XLA Ops:
  2.3 2.9 collective-permute-start
  5.2 2.2 collective-permute-done
  8.4 2.1 collective-permute-start.1
  10.5 2.2 collective-permute-done.1
  12.8 2.1 collective-permute-start.2
  15.8 2.0 collective-permute-done.2
  17.9 4.2 collective-permute-start.3
  22.1 7.4 %collective-permute-done.3 = f32[4,32,32,4]{2,1,3,0:T(8,128)S(1)} collective-permute-done((f32[4,32,32,4]{2,1,3,0:T(8,128)S(1)}, f32[4,32,32,4]{2,1,3,0:T(8,128)S(1)}, u32[]{:S(2)}, u32[]{:S(2)}) %collective-permute-start.3) | collective-permute-done | bytes 65568 | tf_op jit(solution)/shard_map/ppermute | solution.py:36
  32.8 4.0 fusion.343
  49.0 3.0 fusion.344
  56.0 2.0 collective-permute-done.8
  61.8 3.6 fusion.345
  69.4 2.0 collective-permute-done.11
  77.1 3.0 fusion.346
  84.1 2.0 collective-permute-done.14
  89.8 14.0 %fusion.347 = (f32[64]{0:T(128)S(1)}, f32[8,32,32,64]{3,0,2,1:T(8,128)S(1)}) fusion(f32[8,32,32,64]{3,0,2,1:T(8,128)S(1)} %get-tuple-element.370, bf16[2,2,3,3,64,64]{5,4,3,2,1,0:T(8,128)(2,1)S(1)} %get-tuple-element.219, f32[8,32,32,64]{3,0,2,1:T(8,128)S(1)} %get-tuple-element.372, f32[64]{0:T(128)S(1)} %get-tuple-element.255, ...), kind=kOutput, calls=%fused_computation.860 | convolution fusion | flops 584843200 | bytes 10635520 | tf_op jit(solution)/shard_map/conv_general_dilated | solution.py:85
  116.3 47.0 %fusion.61 = f32[8,32,32,6]{0,3,2,1:T(8,128)} fusion(bf16[8,32,32,64]{3,0,2,1:T(8,128)(2,1)S(1)} %multiply_convert_fusion.2, f32[3,3,64,6]{2,3,1,0:T(8,128)S(1)} %copy-done.86), kind=kOutput, calls=%fused_computation.257 | convolution fusion | flops 54291840 | bytes 1259008 | tf_op jit(solution)/shard_map/conv_general_dilated | solution.py:85
  163.4 2.8 copy.247
  175.0 2.0 collective-permute-done.23
  185.9 2.0 collective-permute-done.26
  197.3 2.0 collective-permute-done.29
  221.5 2.2 fusion.352
  226.0 2.7 copy.266
  228.7 3.4 copy.267
  240.9 2.9 collective-permute-start.21
  249.3 2.7 copy.264
  252.0 3.6 copy.265
  260.0 3.2 fusion.49
  263.3 3.0 copy.251
  273.5 2.6 copy.252
  276.1 2.7 multiply_reduce_fusion.14
  280.7 3.0 collective-permute-done.38
  284.3 3.1 collective-permute-done.39
  291.5 3.0 collective-permute-done.41
  295.1 3.1 collective-permute-done.42
  302.8 3.0 collective-permute-done.44
  306.4 3.1 collective-permute-done.45
  310.5 2.2 multiply_reduce_fusion.11
  314.5 3.0 collective-permute-done.47
  318.2 3.1 collective-permute-done.48
  322.2 2.7 multiply_reduce_fusion.10
  327.8 2.2 fusion.354
  333.7 2.9 convolution_bitcast_fusion
  337.8 2.3 fusion.57
  340.1 2.1 copy.253
  345.0 2.5 copy.254
  352.2 7.6 %multiply_reduce_fusion.4 = (f32[64]{0:T(128)S(1)}, f32[64]{0:T(128)S(1)}, f32[8,32,32,64]{3,0,2,1:T(8,128)S(1)}) fusion(f32[8,32,32,64]{3,0,2,1:T(8,128)} %copy-done.3, f32[64]{0:T(128)} %copy-done.136, f32[64]{0:T(128)} %copy-done.134, f32[64]{0:T(128)} %copy-done.190, f32[64]{0:T(128)} %copy-done.201, bf16[8,32,32,6]{0,3,2,1:T(8,128)(2,1)S(1)} %copy.260, ...), kind=kOutput, calls=%fused_computation.13 | convolution fusion | flops 62156032 | bytes 4307968 | tf_op jit(solution)/shard_map/conv_general_dilated | solution.py:85
  371.2 6.9 %multiply_reduce_fusion.3 = (f32[64]{0:T(128)S(1)}, f32[64]{0:T(128)S(1)}, f32[8,32,32,64]{3,0,2,1:T(8,128)S(1)}) fusion(f32[8,32,32,64]{3,0,2,1:T(8,128)S(1)} %copy-done.10, f32[64]{0:T(128)S(1)} %copy-done.194, f32[64]{0:T(128)S(1)} %copy-done.192, f32[64]{0:T(128)S(1)} %copy-done.230, f32[64]{0:T(128)S(1)} %copy-done.232, ...), kind=kOutput, calls=%fused_computation.10 | convolution fusion | flops 587464576 | bytes 10635776 | tf_op jit(solution)/shard_map/conv_general_dilated | solution.py:85
  384.4 85.5 %fusion.353 = f32[3,3,64,6]{3,2,1,0:T(8,128)S(1)} fusion(bf16[8,32,32,64]{3,0,2,1:T(8,128)(2,1)S(1)} %copy-done.53, bf16[8,32,32,6]{0,3,2,1:T(8,128)(2,1)S(1)} %copy.260), kind=kOutput, calls=%fused_computation.866 | convolution fusion | flops 54288384 | bytes 1160704 | tf_op jit(solution)/shard_map/conv_general_dilated | solution.py:97
  472.7 8.2 %multiply_reduce_fusion.2 = (f32[64]{0:T(128)S(1)}, f32[64]{0:T(128)S(1)}, f32[8,32,32,64]{3,0,2,1:T(8,128)}) fusion(f32[8,32,32,64]{3,0,2,1:T(8,128)S(1)} %copy-done.1, f32[64]{0:T(128)S(1)} %copy-done.133, f32[64]{0:T(128)S(1)} %copy-done.131, f32[64]{0:T(128)S(1)} %copy-done.186, f32[64]{0:T(128)S(1)} %copy-done.188, ...), kind=kOutput, calls=%fused_computation.7 | convolution fusion | flops 586940288 | bytes 8538624 | tf_op jit(solution)/shard_map/conv_general_dilated | solution.py:85
  486.7 8.9 %convolution_bitcast_fusion.4 = f32[1,3,3,64,64]{4,3,2,1,0:T(8,128)S(1)} fusion(f32[8,32,32,64]{3,0,2,1:T(8,128)} %copy-done.11, f32[8,32,32,64]{3,0,2,1:T(8,128)} %copy-done.9, f32[64]{0:T(128)S(1)} %copy-done.230, f32[64]{0:T(128)S(1)} %copy-done.232, f32[64]{0:T(128)S(1)} %copy-done.194, f32[64]{0:T(128)S(1)} %copy-done.192), kind=kOutput, calls=%fused_computation.67 | convolution fusion | flops 584318976 | bytes 4342784 | tf_op jit(solution)/shard_map/conv_general_dilated | solution.py:97
  498.6 7.2 %multiply_reduce_fusion.1 = (f32[64]{0:T(128)S(1)}, f32[64]{0:T(128)S(1)}, f32[8,32,32,64]{3,0,2,1:T(8,128)S(1)}) fusion(f32[8,32,32,64]{3,0,2,1:T(8,128)S(1)} %copy-done.8, f32[64]{0:T(128)S(1)} %copy-done.184, f32[64]{0:T(128)S(1)} %copy-done.182, f32[64]{0:T(128)S(1)} %copy-done.226, f32[64]{0:T(128)S(1)} %copy-done.228, ...), kind=kOutput, calls=%fused_computation.4 | convolution fusion | flops 587464576 | bytes 10635776 | tf_op jit(solution)/shard_map/conv_general_dilated | solution.py:85
  505.9 5.1 convolution_bitcast_fusion.5
  512.6 2.0 collective-permute-done.62
  516.3 5.4 convolution_bitcast_fusion.6
  523.3 5.1 convolution_bitcast_fusion.7
  528.5 8.5 %multiply_reduce_fusion = (f32[64]{0:T(128)S(1)}, f32[64]{0:T(128)S(1)}, f32[8,32,32,64]{3,0,2,1:T(8,128)}) fusion(f32[8,32,32,64]{3,0,2,1:T(8,128)S(1)} %copy-done.6, f32[64]{0:T(128)S(1)} %copy-done.176, f32[64]{0:T(128)S(1)} %copy-done.174, f32[64]{0:T(128)S(1)} %copy-done.178, f32[64]{0:T(128)S(1)} %copy-done.180, ...), kind=kOutput, calls=%fused_computation.1 | convolution fusion | flops 586940288 | bytes 8538624 | tf_op jit(solution)/shard_map/conv_general_dilated | solution.py:85
  543.0 2.6 collective-permute-done.66
  546.3 7.4 %fusion.7 = f32[1,3,3,6,64]{4,3,2,1,0:T(8,128)S(1)} fusion(bf16[8,32,32,6]{0,3,2,1:T(8,128)(2,1)} %copy-done.47, f32[8,32,32,64]{3,0,2,1:T(8,128)} %copy-done.32, f32[8,32,32,64]{3,0,2,1:T(8,128)} %get-tuple-element.394, f32[8,32,32,64]{3,0,2,1:T(8,128)} %copy-done.5, f32[64]{0:T(128)S(1)} %get-tuple-element.324, f32[64]{0:T(128)S(1)} %get-tuple-element.323, ...), kind=kOutput, calls=%fused_computation.71 | convolution fusion | flops 59006976 | bytes 6404864 | tf_op jit(solution)/shard_map/conv_general_dilated | solution.py:97
  554.0 5.2 concatenate.48
  559.3 2.9 collective-permute-done.67
  564.0 28.0 %collective-permute-done.68 = f32[2440,128]{1,0:T(8,128)S(1)} collective-permute-done((f32[2440,128]{1,0:T(8,128)S(1)}, f32[2440,128]{1,0:T(8,128)S(1)}, u32[]{:S(2)}, u32[]{:S(2)}) %collective-permute-start.68) | collective-permute-done | bytes 1249312 | tf_op jit(solution)/shard_map/ppermute | solution.py:36
  593.4 27.5 %collective-permute-done.69 = f32[2440,128]{1,0:T(8,128)S(1)} collective-permute-done((f32[2440,128]{1,0:T(8,128)S(1)}, f32[2440,128]{1,0:T(8,128)S(1)}, u32[]{:S(2)}, u32[]{:S(2)}) %collective-permute-start.69) | collective-permute-done | bytes 1249312 | tf_op jit(solution)/shard_map/ppermute | solution.py:36
  640.1 8.0 %fusion.334 = (bf16[2,2,2,3,3,64,64]{6,5,4,3,2,1,0:T(8,128)(2,1)}, f32[2,2,2,3,3,64,64]{6,5,4,3,2,1,0:T(8,128)}, f32[2,2,2,3,3,64,64]{6,5,4,3,2,1,0:T(8,128)}, f32[2,2,2,3,3,64,64]{6,5,4,3,2,1,0:T(8,128)}) fusion(f32[2,2,2,3,3,64,64]{6,5,4,3,2,1,0:T(8,128)S(1)} %copy-done.14, f32[2,2,2,3,3,64,64]{6,5,4,3,2,1,0:T(8,128)} %reshape.2136, ...), kind=kLoop, calls=%fused_computation.852 | loop fusion | flops 4423680 | bytes 8847360 | tf_op jit(solution)/shard_map/convert_element_type | solution.py:185
  (847 shorter events, 223.2 us)
Async XLA Ops:
  2.3 5.2 collective-permute-start
  8.4 4.4 collective-permute-start.1
  12.8 5.1 collective-permute-start.2
  17.9 11.6 %collective-permute-start.3 = (f32[4,32,32,4]{2,1,3,0:T(8,128)S(1)}, f32[4,32,32,4]{2,1,3,0:T(8,128)S(1)}, u32[]{:S(2)}, u32[]{:S(2)}) collective-permute-start(f32[4,32,32,4]{2,1,3,0:T(8,128)S(1)} %pad_maximum_fusion.6), channel_id=1, source_target_pairs={{0,4},{1,5},{2,6},{3,7},{4,0},{5,1},{6,2},{7,3},{8,12},{9,13},{10,... | collective-permute-start | bytes 196616 | tf_op jit(solution)/shard_map/ppermute | solution.py:36
  38.0 2.3 collective-permute-start.4
  40.3 3.6 collective-permute-start.5
  44.0 3.6 collective-permute-start.6
  54.4 3.6 collective-permute-start.8
  58.1 3.6 collective-permute-start.9
  66.6 1.2 collective-permute-start.10
  67.8 3.6 collective-permute-start.11
  71.5 3.6 collective-permute-start.12
  81.2 1.2 collective-permute-start.13
  82.5 3.6 collective-permute-start.14
  86.1 3.6 collective-permute-start.15
  105.0 1.2 collective-permute-start.16
  106.3 3.6 collective-permute-start.17
  109.9 3.6 collective-permute-start.18
  173.4 3.6 collective-permute-start.23
  177.1 3.6 collective-permute-start.24
  183.1 1.2 collective-permute-start.25
  184.3 3.6 collective-permute-start.26
  188.0 3.6 collective-permute-start.27
  194.5 1.2 collective-permute-start.28
  195.7 3.6 collective-permute-start.29
  199.4 3.6 collective-permute-start.30
  208.0 4.6 collective-permute-start.31
  213.4 3.6 collective-permute-start.32
  217.0 3.6 collective-permute-start.33
  224.7 7.4 %collective-permute-start.34 = (f32[2,64]{1,0:T(2,128)}, f32[2,64]{1,0:T(2,128)}, u32[]{:S(2)}, u32[]{:S(2)}) collective-permute-start(f32[2,64]{1,0:T(2,128)} %pad_maximum_fusion.38), channel_id=1, source_target_pairs={{0,1},{1,0},{2,3},{3,2},{4,5},{5,4},{6,7},{7,6},{8,9},{9,8},{10,11... | collective-permute-start | bytes 1544 | tf_op jit(solution)/shard_map/ppermute | solution.py:36
  225.5 9.9 %collective-permute-start.19 = (f32[1]{0:T(128)}, f32[1]{0:T(128)}, u32[]{:S(2)}, u32[]{:S(2)}) collective-permute-start(f32[1]{0:T(128)} %bitcast.62), channel_id=1, source_target_pairs={{0,1},{1,0},{2,3},{3,2},{4,5},{5,4},{6,7},{7,6},{8,9},{9,8},{10,11... | collective-permute-start | bytes 20 | tf_op jit(solution)/shard_map/ppermute | solution.py:36
  233.9 11.2 %collective-permute-start.35 = (f32[2,64]{1,0:T(2,128)}, f32[2,64]{1,0:T(2,128)}, u32[]{:S(2)}, u32[]{:S(2)}) collective-permute-start(f32[2,64]{1,0:T(2,128)} %pad_maximum_fusion.39), channel_id=1, source_target_pairs={{0,8},{8,0},{16,24},{24,16},{1,9},{9,1},{17,25},{25,17},{2,10},{10... | collective-permute-start | bytes 1544 | tf_op jit(solution)/shard_map/ppermute | solution.py:36
  236.7 3.6 collective-permute-start.20
  240.9 3.6 collective-permute-start.21
  246.4 9.1 %collective-permute-start.36 = (f32[2,64]{1,0:T(2,128)}, f32[2,64]{1,0:T(2,128)}, u32[]{:S(2)}, u32[]{:S(2)}) collective-permute-start(f32[2,64]{1,0:T(2,128)} %pad_maximum_fusion.40), channel_id=1, source_target_pairs={{0,16},{8,24},{16,0},{24,8},{1,17},{9,25},{17,1},{25,9},{2,18},{10... | collective-permute-start | bytes 1544 | tf_op jit(solution)/shard_map/ppermute | solution.py:36
  278.9 1.2 collective-permute-start.37
  280.1 3.6 collective-permute-start.38
  283.8 3.6 collective-permute-start.39
  289.7 1.2 collective-permute-start.40
  290.9 3.6 collective-permute-start.41
  294.5 3.6 collective-permute-start.42
  301.0 1.2 collective-permute-start.43
  302.2 3.6 collective-permute-start.44
  305.9 3.6 collective-permute-start.45
  313.9 3.6 collective-permute-start.47
  317.6 3.6 collective-permute-start.48
  327.3 5.1 collective-permute-start.50
  333.2 3.6 collective-permute-start.51
  359.8 1.5 collective-permute-start.52
  361.4 3.6 collective-permute-start.53
  365.1 3.6 collective-permute-start.54
  379.3 3.6 collective-permute-start.56
  383.0 86.9 %collective-permute-start.57 = (f32[2,64]{1,0:T(2,128)S(1)}, f32[2,64]{1,0:T(2,128)S(1)}, u32[]{:S(2)}, u32[]{:S(2)}) collective-permute-start(f32[2,64]{1,0:T(2,128)S(1)} %fusion.389), channel_id=1, source_target_pairs={{0,16},{8,24},{16,0},{24,8},{1,17},{9,25},{17,1},{25,9},{2,18},{10... | collective-permute-start | bytes 1544 | tf_op jit(solution)/shard_map/ppermute | solution.py:36
  481.0 1.2 collective-permute-start.58
  482.2 3.6 collective-permute-start.59
  485.9 9.7 %collective-permute-start.60 = (f32[2,64]{1,0:T(2,128)S(1)}, f32[2,64]{1,0:T(2,128)S(1)}, u32[]{:S(2)}, u32[]{:S(2)}) collective-permute-start(f32[2,64]{1,0:T(2,128)S(1)} %fusion.388), channel_id=1, source_target_pairs={{0,16},{8,24},{16,0},{24,8},{1,17},{9,25},{17,1},{25,9},{2,18},{10... | collective-permute-start | bytes 1544 | tf_op jit(solution)/shard_map/ppermute | solution.py:36
  505.8 5.2 collective-permute-start.61
  511.0 3.6 collective-permute-start.62
  514.6 7.0 %collective-permute-start.63 = (f32[2,64]{1,0:T(2,128)S(1)}, f32[2,64]{1,0:T(2,128)S(1)}, u32[]{:S(2)}, u32[]{:S(2)}) collective-permute-start(f32[2,64]{1,0:T(2,128)S(1)} %fusion.387), channel_id=1, source_target_pairs={{0,16},{8,24},{16,0},{24,8},{1,17},{9,25},{17,1},{25,9},{2,18},{10... | collective-permute-start | bytes 1544 | tf_op jit(solution)/shard_map/ppermute | solution.py:36
  538.2 3.6 collective-permute-start.65
  541.9 3.7 collective-permute-start.66
  559.2 3.0 collective-permute-start.67
  562.4 29.6 %collective-permute-start.68 = (f32[2440,128]{1,0:T(8,128)S(1)}, f32[2440,128]{1,0:T(8,128)S(1)}, u32[]{:S(2)}, u32[]{:S(2)}) collective-permute-start(f32[2440,128]{1,0:T(8,128)S(1)} %bitcast_add_fusion.110), channel_id=1, source_target_pairs={{0,8},{8,0},{16,24},{24,16},{1,9},{9,1},{17,25},{25,17},{2,10},{10... | collective-permute-start | bytes 3747848 | tf_op jit(solution)/shard_map/ppermute | solution.py:36
  592.1 28.7 %collective-permute-start.69 = (f32[2440,128]{1,0:T(8,128)S(1)}, f32[2440,128]{1,0:T(8,128)S(1)}, u32[]{:S(2)}, u32[]{:S(2)}) collective-permute-start(f32[2440,128]{1,0:T(8,128)S(1)} %fusion.385), channel_id=1, source_target_pairs={{0,16},{8,24},{16,0},{24,8},{1,17},{9,25},{17,1},{25,9},{2,18},{10... | collective-permute-start | bytes 3747848 | tf_op jit(solution)/shard_map/ppermute | solution.py:36
  (249 other events, 2546.7 us)
